TPU v7x, 32 devices: a whole 2x2x4 slice. The times are simulated.
32 devices in a mesh: ctx: 8 (over z, x), head: 4 (over y, core).
Axes of the slice: x: 2, y: 2, z: 4, core: 2. Of those that a mesh axis runs over, the one named last changes fastest.
Arguments:
- queries: bfloat16 [2048, 2048], P('ctx', 'head'), may hold values from -110 to 110
- keys: bfloat16 [32768, 128], P('ctx'), may hold values from -6 to 6
- values: bfloat16 [32768, 128], P('ctx'), may hold values from -6 to 6
- w_out: bfloat16 [2048, 16384], P(None, 'head'), may hold values from -0.125 to 0.125
- new_counts: int32 [8], replicated, may hold values from 1 to 1024, as said below
- prior_lengths: int32 [8], replicated, may hold values from 1 to 15360, as said below
Outputs:
- mixed: bfloat16 [2048, 16384], P('ctx', 'head')
Inputs may be any that keep to these rules, and one draw needn't show every extreme that they name: `new_counts`: every request has at least one new token; the counts add up to 2048. `prior_lengths`: every request has at least one cached token; the lengths add up to 30720.
All inputs are finite; a program needn't handle non-finite values.
Results may differ from a plain program's by a relative error of at most 0.011.
Values may be sent and summed in bfloat16 or wider, within the bound.
No kernel may reach another device: no remote copies, remote signals or barrier semaphores. Data moves between devices by JAX's collectives and lax.ppermute only.
A program may use at most 384 MiB of HBM per device.

v0:
```python
import jax
import jax.numpy as jnp
from jax import lax
from jax.sharding import PartitionSpec as P

NEG = -1e30


def from_behind(value, axis, steps):
    count = lax.axis_size(axis)
    pairs = [(source, (source + steps) % count) for source in range(count)]
    return lax.ppermute(value, axis, pairs)


def row_info(index, ends, table):
    req = jnp.sum((index[:, None] >= ends[None, :]).astype(jnp.int32), axis=1)
    onehot = (req[:, None] == jnp.arange(ends.shape[0], dtype=jnp.int32)[None, :]).astype(jnp.int32)
    return (req, index + jnp.sum(onehot * table[None, :], axis=1))


def partial_block(q_block, q_req, q_pos, key_rows, value_rows, k_req, k_pos):
    count = q_block.shape[0]
    width = key_rows.shape[1]
    heads = q_block.shape[1] // width
    q_three = q_block.reshape(count, heads, width)
    scores = jnp.einsum(
        "nhd,kd->nhk", q_three, key_rows, preferred_element_type=jnp.float32
    ) * width ** (-0.5)
    allowed = ((q_req[:, None] == k_req[None, :]) & (k_pos[None, :] <= q_pos[:, None]))[:, None, :]
    scores = jnp.where(allowed, scores, NEG)
    top = jnp.max(scores, axis=2)
    weights = jnp.where(allowed, jnp.exp(scores - top[:, :, None]), 0.0)
    total = jnp.sum(weights, axis=2)
    summed = jnp.einsum(
        "nhk,kd->nhd", weights.astype(jnp.bfloat16), value_rows, preferred_element_type=jnp.float32
    )
    live = total > 0.0
    safe = jnp.where(live, total, 1.0)
    return (summed / safe[:, :, None], jnp.where(live, top + jnp.log(safe), NEG))


def merge_pair(out_one, lse_one, out_two, lse_two):
    top = jnp.maximum(lse_one, lse_two)
    left = jnp.exp(lse_one - top)
    right = jnp.exp(lse_two - top)
    total = left + right
    merged = (left[:, :, None] * out_one + right[:, :, None] * out_two) / total[:, :, None]
    return (merged, top + jnp.log(total))


def body(queries, keys, values, w_out, new_counts, prior_lengths):
    ctx_count = lax.axis_size("ctx")
    device = lax.axis_index("ctx")
    rows = queries.shape[0]
    cache = keys.shape[0]
    width = keys.shape[1]
    heads = queries.shape[1] // width
    q_ends = jnp.cumsum(new_counts)
    q_table = prior_lengths - (q_ends - new_counts)
    spans = new_counts + prior_lengths
    k_ends = jnp.cumsum(spans)
    k_table = spans - k_ends

    def query_info(block):
        return row_info(block * rows + jnp.arange(rows, dtype=jnp.int32), q_ends, q_table)

    empty_out = jnp.zeros((rows, heads, width), jnp.float32)
    empty_lse = jnp.full((rows, heads), NEG, jnp.float32)
    k_req, k_pos = row_info(device * cache + jnp.arange(cache, dtype=jnp.int32), k_ends, k_table)

    def step(turn, state):
        q_now, out, lse = state
        anchor = (device - turn) % ctx_count
        q_req, q_pos = query_info(anchor)
        part_out, part_lse = partial_block(q_now, q_req, q_pos, keys, values, k_req, k_pos)
        out, lse = merge_pair(out, lse, part_out, part_lse)
        q_now = from_behind(q_now, "ctx", 1)
        out, lse = from_behind((out, lse), "ctx", 1)
        return (q_now, out, lse)

    last = lax.fori_loop(0, ctx_count, step, (queries, empty_out, empty_lse))
    out = last[1]
    attended = out.reshape(rows, heads * width).astype(jnp.bfloat16)
    mixed = jnp.dot(
        lax.all_gather(attended, "head", axis=1, tiled=True),
        w_out,
        preferred_element_type=jnp.float32,
    )
    return mixed.astype(jnp.bfloat16)


def solution(mesh):
    return jax.shard_map(
        body,
        mesh=mesh,
        in_specs=(P("ctx", "head"), P("ctx", None), P("ctx", None), P(None, "head"), P(), P()),
        out_specs=P("ctx", "head"),
        check_vma=False,
    )
```

profile of v0, /device:TPU:0, one launch (start us, length us, event | category | flops | bytes accessed | tf_op | source)
XLA Modules:
  0.0 337.0 jit_solution(3748461697291333664)
XLA Ops:
  6.5 0.9 copy.34
  9.5 295.1 %while.19 = (s32[]{:T(128)}, bf16[256,512]{1,0:T(8,128)(2,1)S(1)}, f32[256,4,128]{2,0,1:T(8,128)S(1)}, f32[256,4]{0,1:T(4,128)S(1)}, s32[]{:T(128)}, /*index=5*/...) while((s32[]{:T(128)}, bf16[256,512]{1,0:T(8,128)(2,1)S(1)}, ...), condition=%wide.region_9.10_spmd, body=%wide.region_4.9_spmd.sunk | while | flops 2205830400 | bytes 65922548 | solution.py:81
  9.7 0.9 compare_and_fusion.2
  10.7 4.8 %fusion.51 = (f32[256,4]{0,1:T(4,128)S(1)}, f32[256,4,4096]{2,0,1:T(8,128)S(1)}) fusion(pred[256,4096]{1,0:T(8,128)(4,1)S(1)} %compare_and_fusion.2, bf16[4096,128]{1,0:T(8,128)(2,1)} %get-tuple-element.424, bf16[256,512]{1,0:T(8,128)(2,1)S(1)} %copy.26), kind=kOutput, calls=%fused_computation.2.clone.1 | convolution fusion | flops 1086323712 | bytes 19140608 | tf_op jit(solution)/shard_map/while/body/eval_jaxpr/nhd,kd->nhk/dot_general | solution.py:26
  15.5 5.0 %fusion.52 = f32[256,4]{0,1:T(4,128)S(1)} fusion(f32[256,4,4096]{2,0,1:T(8,128)S(1)} %get-tuple-element.376, f32[256,4]{0,1:T(4,128)S(1)} %get-tuple-element.377, pred[256,4096]{1,0:T(8,128)(4,1)S(1)} %compare_and_fusion.2), kind=kLoop, calls=%fused_computation.4.clone.1 | loop fusion | flops 20970496 | bytes 17833984 | tf_op jit(solution)/shard_map/while/body/eval_jaxpr/reduce_sum | solution.py:33
  20.5 6.4 %fusion.53 = f32[256,4,128]{2,0,1:T(8,128)S(1)} fusion(bf16[4096,128]{1,0:T(8,128)(2,1)S(1)} %copy-done, f32[256,4,4096]{2,0,1:T(8,128)S(1)} %get-tuple-element.376, f32[256,4]{0,1:T(4,128)S(1)} %get-tuple-element.377, pred[256,4096]{1,0:T(8,128)(4,1)S(1)} %compare_and_fusion.2, f32[256,4,128]{2,0,1:T(8,128)S(1)} %get-tuple-element.401, ...), kind=kOutput, calls=%fused_computation.14.clone.1 | convolution fusion | flops 1095368704 | bytes 19943424 | tf_op jit(solution)/shard_map/while/body/eval_jaxpr/nhk,kd->nhd/dot_general | solution.py:34
  27.0 3.0 collective-permute-start.1
  30.0 1.6 collective-permute-start
  31.5 1.5 collective-permute-start.2
  33.0 17.6 %collective-permute-done.2 = f32[256,4]{0,1:T(4,128)S(1)} collective-permute-done((f32[256,4]{0,1:T(4,128)S(1)}, f32[256,4]{0,1:T(4,128)S(1)}, u32[]{:S(2)}, u32[]{:S(2)}) %collective-permute-start.2) | collective-permute-done | bytes 4128 | tf_op jit(solution)/shard_map/while/body/eval_jaxpr/ppermute | solution.py:12
  50.9 0.9 compare_and_fusion.2
  51.8 4.8 %fusion.51 = (f32[256,4]{0,1:T(4,128)S(1)}, f32[256,4,4096]{2,0,1:T(8,128)S(1)}) fusion(pred[256,4096]{1,0:T(8,128)(4,1)S(1)} %compare_and_fusion.2, bf16[4096,128]{1,0:T(8,128)(2,1)} %get-tuple-element.424, bf16[256,512]{1,0:T(8,128)(2,1)S(1)} %copy.26), kind=kOutput, calls=%fused_computation.2.clone.1 | convolution fusion | flops 1086323712 | bytes 19140608 | tf_op jit(solution)/shard_map/while/body/eval_jaxpr/nhd,kd->nhk/dot_general | solution.py:26
  56.6 5.0 %fusion.52 = f32[256,4]{0,1:T(4,128)S(1)} fusion(f32[256,4,4096]{2,0,1:T(8,128)S(1)} %get-tuple-element.376, f32[256,4]{0,1:T(4,128)S(1)} %get-tuple-element.377, pred[256,4096]{1,0:T(8,128)(4,1)S(1)} %compare_and_fusion.2), kind=kLoop, calls=%fused_computation.4.clone.1 | loop fusion | flops 20970496 | bytes 17833984 | tf_op jit(solution)/shard_map/while/body/eval_jaxpr/reduce_sum | solution.py:33
  61.7 6.4 %fusion.53 = f32[256,4,128]{2,0,1:T(8,128)S(1)} fusion(bf16[4096,128]{1,0:T(8,128)(2,1)S(1)} %copy-done, f32[256,4,4096]{2,0,1:T(8,128)S(1)} %get-tuple-element.376, f32[256,4]{0,1:T(4,128)S(1)} %get-tuple-element.377, pred[256,4096]{1,0:T(8,128)(4,1)S(1)} %compare_and_fusion.2, f32[256,4,128]{2,0,1:T(8,128)S(1)} %get-tuple-element.401, ...), kind=kOutput, calls=%fused_computation.14.clone.1 | convolution fusion | flops 1095368704 | bytes 19943424 | tf_op jit(solution)/shard_map/while/body/eval_jaxpr/nhk,kd->nhd/dot_general | solution.py:34
  68.2 1.1 collective-permute-start
  69.9 19.8 %collective-permute-done.2 = f32[256,4]{0,1:T(4,128)S(1)} collective-permute-done((f32[256,4]{0,1:T(4,128)S(1)}, f32[256,4]{0,1:T(4,128)S(1)}, u32[]{:S(2)}, u32[]{:S(2)}) %collective-permute-start.2) | collective-permute-done | bytes 4128 | tf_op jit(solution)/shard_map/while/body/eval_jaxpr/ppermute | solution.py:12
  89.9 0.9 compare_and_fusion.2
  90.8 4.8 %fusion.51 = (f32[256,4]{0,1:T(4,128)S(1)}, f32[256,4,4096]{2,0,1:T(8,128)S(1)}) fusion(pred[256,4096]{1,0:T(8,128)(4,1)S(1)} %compare_and_fusion.2, bf16[4096,128]{1,0:T(8,128)(2,1)} %get-tuple-element.424, bf16[256,512]{1,0:T(8,128)(2,1)S(1)} %copy.26), kind=kOutput, calls=%fused_computation.2.clone.1 | convolution fusion | flops 1086323712 | bytes 19140608 | tf_op jit(solution)/shard_map/while/body/eval_jaxpr/nhd,kd->nhk/dot_general | solution.py:26
  95.6 5.0 %fusion.52 = f32[256,4]{0,1:T(4,128)S(1)} fusion(f32[256,4,4096]{2,0,1:T(8,128)S(1)} %get-tuple-element.376, f32[256,4]{0,1:T(4,128)S(1)} %get-tuple-element.377, pred[256,4096]{1,0:T(8,128)(4,1)S(1)} %compare_and_fusion.2), kind=kLoop, calls=%fused_computation.4.clone.1 | loop fusion | flops 20970496 | bytes 17833984 | tf_op jit(solution)/shard_map/while/body/eval_jaxpr/reduce_sum | solution.py:33
  100.7 6.4 %fusion.53 = f32[256,4,128]{2,0,1:T(8,128)S(1)} fusion(bf16[4096,128]{1,0:T(8,128)(2,1)S(1)} %copy-done, f32[256,4,4096]{2,0,1:T(8,128)S(1)} %get-tuple-element.376, f32[256,4]{0,1:T(4,128)S(1)} %get-tuple-element.377, pred[256,4096]{1,0:T(8,128)(4,1)S(1)} %compare_and_fusion.2, f32[256,4,128]{2,0,1:T(8,128)S(1)} %get-tuple-element.401, ...), kind=kOutput, calls=%fused_computation.14.clone.1 | convolution fusion | flops 1095368704 | bytes 19943424 | tf_op jit(solution)/shard_map/while/body/eval_jaxpr/nhk,kd->nhd/dot_general | solution.py:34
  107.4 20.4 %collective-permute-done.2 = f32[256,4]{0,1:T(4,128)S(1)} collective-permute-done((f32[256,4]{0,1:T(4,128)S(1)}, f32[256,4]{0,1:T(4,128)S(1)}, u32[]{:S(2)}, u32[]{:S(2)}) %collective-permute-start.2) | collective-permute-done | bytes 4128 | tf_op jit(solution)/shard_map/while/body/eval_jaxpr/ppermute | solution.py:12
  128.0 0.9 compare_and_fusion.2
  129.0 4.8 %fusion.51 = (f32[256,4]{0,1:T(4,128)S(1)}, f32[256,4,4096]{2,0,1:T(8,128)S(1)}) fusion(pred[256,4096]{1,0:T(8,128)(4,1)S(1)} %compare_and_fusion.2, bf16[4096,128]{1,0:T(8,128)(2,1)} %get-tuple-element.424, bf16[256,512]{1,0:T(8,128)(2,1)S(1)} %copy.26), kind=kOutput, calls=%fused_computation.2.clone.1 | convolution fusion | flops 1086323712 | bytes 19140608 | tf_op jit(solution)/shard_map/while/body/eval_jaxpr/nhd,kd->nhk/dot_general | solution.py:26
  133.8 5.0 %fusion.52 = f32[256,4]{0,1:T(4,128)S(1)} fusion(f32[256,4,4096]{2,0,1:T(8,128)S(1)} %get-tuple-element.376, f32[256,4]{0,1:T(4,128)S(1)} %get-tuple-element.377, pred[256,4096]{1,0:T(8,128)(4,1)S(1)} %compare_and_fusion.2), kind=kLoop, calls=%fused_computation.4.clone.1 | loop fusion | flops 20970496 | bytes 17833984 | tf_op jit(solution)/shard_map/while/body/eval_jaxpr/reduce_sum | solution.py:33
  138.8 6.4 %fusion.53 = f32[256,4,128]{2,0,1:T(8,128)S(1)} fusion(bf16[4096,128]{1,0:T(8,128)(2,1)S(1)} %copy-done, f32[256,4,4096]{2,0,1:T(8,128)S(1)} %get-tuple-element.376, f32[256,4]{0,1:T(4,128)S(1)} %get-tuple-element.377, pred[256,4096]{1,0:T(8,128)(4,1)S(1)} %compare_and_fusion.2, f32[256,4,128]{2,0,1:T(8,128)S(1)} %get-tuple-element.401, ...), kind=kOutput, calls=%fused_computation.14.clone.1 | convolution fusion | flops 1095368704 | bytes 19943424 | tf_op jit(solution)/shard_map/while/body/eval_jaxpr/nhk,kd->nhd/dot_general | solution.py:34
  145.5 19.5 %collective-permute-done.2 = f32[256,4]{0,1:T(4,128)S(1)} collective-permute-done((f32[256,4]{0,1:T(4,128)S(1)}, f32[256,4]{0,1:T(4,128)S(1)}, u32[]{:S(2)}, u32[]{:S(2)}) %collective-permute-start.2) | collective-permute-done | bytes 4128 | tf_op jit(solution)/shard_map/while/body/eval_jaxpr/ppermute | solution.py:12
  165.2 0.9 compare_and_fusion.2
  166.2 4.8 %fusion.51 = (f32[256,4]{0,1:T(4,128)S(1)}, f32[256,4,4096]{2,0,1:T(8,128)S(1)}) fusion(pred[256,4096]{1,0:T(8,128)(4,1)S(1)} %compare_and_fusion.2, bf16[4096,128]{1,0:T(8,128)(2,1)} %get-tuple-element.424, bf16[256,512]{1,0:T(8,128)(2,1)S(1)} %copy.26), kind=kOutput, calls=%fused_computation.2.clone.1 | convolution fusion | flops 1086323712 | bytes 19140608 | tf_op jit(solution)/shard_map/while/body/eval_jaxpr/nhd,kd->nhk/dot_general | solution.py:26
  170.9 5.0 %fusion.52 = f32[256,4]{0,1:T(4,128)S(1)} fusion(f32[256,4,4096]{2,0,1:T(8,128)S(1)} %get-tuple-element.376, f32[256,4]{0,1:T(4,128)S(1)} %get-tuple-element.377, pred[256,4096]{1,0:T(8,128)(4,1)S(1)} %compare_and_fusion.2), kind=kLoop, calls=%fused_computation.4.clone.1 | loop fusion | flops 20970496 | bytes 17833984 | tf_op jit(solution)/shard_map/while/body/eval_jaxpr/reduce_sum | solution.py:33
  176.0 6.4 %fusion.53 = f32[256,4,128]{2,0,1:T(8,128)S(1)} fusion(bf16[4096,128]{1,0:T(8,128)(2,1)S(1)} %copy-done, f32[256,4,4096]{2,0,1:T(8,128)S(1)} %get-tuple-element.376, f32[256,4]{0,1:T(4,128)S(1)} %get-tuple-element.377, pred[256,4096]{1,0:T(8,128)(4,1)S(1)} %compare_and_fusion.2, f32[256,4,128]{2,0,1:T(8,128)S(1)} %get-tuple-element.401, ...), kind=kOutput, calls=%fused_computation.14.clone.1 | convolution fusion | flops 1095368704 | bytes 19943424 | tf_op jit(solution)/shard_map/while/body/eval_jaxpr/nhk,kd->nhd/dot_general | solution.py:34
  182.7 18.6 %collective-permute-done.2 = f32[256,4]{0,1:T(4,128)S(1)} collective-permute-done((f32[256,4]{0,1:T(4,128)S(1)}, f32[256,4]{0,1:T(4,128)S(1)}, u32[]{:S(2)}, u32[]{:S(2)}) %collective-permute-start.2) | collective-permute-done | bytes 4128 | tf_op jit(solution)/shard_map/while/body/eval_jaxpr/ppermute | solution.py:12
  201.5 0.9 compare_and_fusion.2
  202.4 4.8 %fusion.51 = (f32[256,4]{0,1:T(4,128)S(1)}, f32[256,4,4096]{2,0,1:T(8,128)S(1)}) fusion(pred[256,4096]{1,0:T(8,128)(4,1)S(1)} %compare_and_fusion.2, bf16[4096,128]{1,0:T(8,128)(2,1)} %get-tuple-element.424, bf16[256,512]{1,0:T(8,128)(2,1)S(1)} %copy.26), kind=kOutput, calls=%fused_computation.2.clone.1 | convolution fusion | flops 1086323712 | bytes 19140608 | tf_op jit(solution)/shard_map/while/body/eval_jaxpr/nhd,kd->nhk/dot_general | solution.py:26
  207.2 5.0 %fusion.52 = f32[256,4]{0,1:T(4,128)S(1)} fusion(f32[256,4,4096]{2,0,1:T(8,128)S(1)} %get-tuple-element.376, f32[256,4]{0,1:T(4,128)S(1)} %get-tuple-element.377, pred[256,4096]{1,0:T(8,128)(4,1)S(1)} %compare_and_fusion.2), kind=kLoop, calls=%fused_computation.4.clone.1 | loop fusion | flops 20970496 | bytes 17833984 | tf_op jit(solution)/shard_map/while/body/eval_jaxpr/reduce_sum | solution.py:33
  212.3 6.4 %fusion.53 = f32[256,4,128]{2,0,1:T(8,128)S(1)} fusion(bf16[4096,128]{1,0:T(8,128)(2,1)S(1)} %copy-done, f32[256,4,4096]{2,0,1:T(8,128)S(1)} %get-tuple-element.376, f32[256,4]{0,1:T(4,128)S(1)} %get-tuple-element.377, pred[256,4096]{1,0:T(8,128)(4,1)S(1)} %compare_and_fusion.2, f32[256,4,128]{2,0,1:T(8,128)S(1)} %get-tuple-element.401, ...), kind=kOutput, calls=%fused_computation.14.clone.1 | convolution fusion | flops 1095368704 | bytes 19943424 | tf_op jit(solution)/shard_map/while/body/eval_jaxpr/nhk,kd->nhd/dot_general | solution.py:34
  218.9 17.7 %collective-permute-done.2 = f32[256,4]{0,1:T(4,128)S(1)} collective-permute-done((f32[256,4]{0,1:T(4,128)S(1)}, f32[256,4]{0,1:T(4,128)S(1)}, u32[]{:S(2)}, u32[]{:S(2)}) %collective-permute-start.2) | collective-permute-done | bytes 4128 | tf_op jit(solution)/shard_map/while/body/eval_jaxpr/ppermute | solution.py:12
  236.8 0.9 compare_and_fusion.2
  237.8 4.8 %fusion.51 = (f32[256,4]{0,1:T(4,128)S(1)}, f32[256,4,4096]{2,0,1:T(8,128)S(1)}) fusion(pred[256,4096]{1,0:T(8,128)(4,1)S(1)} %compare_and_fusion.2, bf16[4096,128]{1,0:T(8,128)(2,1)} %get-tuple-element.424, bf16[256,512]{1,0:T(8,128)(2,1)S(1)} %copy.26), kind=kOutput, calls=%fused_computation.2.clone.1 | convolution fusion | flops 1086323712 | bytes 19140608 | tf_op jit(solution)/shard_map/while/body/eval_jaxpr/nhd,kd->nhk/dot_general | solution.py:26
  242.6 5.0 %fusion.52 = f32[256,4]{0,1:T(4,128)S(1)} fusion(f32[256,4,4096]{2,0,1:T(8,128)S(1)} %get-tuple-element.376, f32[256,4]{0,1:T(4,128)S(1)} %get-tuple-element.377, pred[256,4096]{1,0:T(8,128)(4,1)S(1)} %compare_and_fusion.2), kind=kLoop, calls=%fused_computation.4.clone.1 | loop fusion | flops 20970496 | bytes 17833984 | tf_op jit(solution)/shard_map/while/body/eval_jaxpr/reduce_sum | solution.py:33
  247.7 6.4 %fusion.53 = f32[256,4,128]{2,0,1:T(8,128)S(1)} fusion(bf16[4096,128]{1,0:T(8,128)(2,1)S(1)} %copy-done, f32[256,4,4096]{2,0,1:T(8,128)S(1)} %get-tuple-element.376, f32[256,4]{0,1:T(4,128)S(1)} %get-tuple-element.377, pred[256,4096]{1,0:T(8,128)(4,1)S(1)} %compare_and_fusion.2, f32[256,4,128]{2,0,1:T(8,128)S(1)} %get-tuple-element.401, ...), kind=kOutput, calls=%fused_computation.14.clone.1 | convolution fusion | flops 1095368704 | bytes 19943424 | tf_op jit(solution)/shard_map/while/body/eval_jaxpr/nhk,kd->nhd/dot_general | solution.py:34
  254.3 16.7 %collective-permute-done.2 = f32[256,4]{0,1:T(4,128)S(1)} collective-permute-done((f32[256,4]{0,1:T(4,128)S(1)}, f32[256,4]{0,1:T(4,128)S(1)}, u32[]{:S(2)}, u32[]{:S(2)}) %collective-permute-start.2) | collective-permute-done | bytes 4128 | tf_op jit(solution)/shard_map/while/body/eval_jaxpr/ppermute | solution.py:12
  271.3 0.9 compare_and_fusion.2
  272.2 4.8 %fusion.51 = (f32[256,4]{0,1:T(4,128)S(1)}, f32[256,4,4096]{2,0,1:T(8,128)S(1)}) fusion(pred[256,4096]{1,0:T(8,128)(4,1)S(1)} %compare_and_fusion.2, bf16[4096,128]{1,0:T(8,128)(2,1)} %get-tuple-element.424, bf16[256,512]{1,0:T(8,128)(2,1)S(1)} %copy.26), kind=kOutput, calls=%fused_computation.2.clone.1 | convolution fusion | flops 1086323712 | bytes 19140608 | tf_op jit(solution)/shard_map/while/body/eval_jaxpr/nhd,kd->nhk/dot_general | solution.py:26
  277.0 5.0 %fusion.52 = f32[256,4]{0,1:T(4,128)S(1)} fusion(f32[256,4,4096]{2,0,1:T(8,128)S(1)} %get-tuple-element.376, f32[256,4]{0,1:T(4,128)S(1)} %get-tuple-element.377, pred[256,4096]{1,0:T(8,128)(4,1)S(1)} %compare_and_fusion.2), kind=kLoop, calls=%fused_computation.4.clone.1 | loop fusion | flops 20970496 | bytes 17833984 | tf_op jit(solution)/shard_map/while/body/eval_jaxpr/reduce_sum | solution.py:33
  282.1 6.4 %fusion.53 = f32[256,4,128]{2,0,1:T(8,128)S(1)} fusion(bf16[4096,128]{1,0:T(8,128)(2,1)S(1)} %copy-done, f32[256,4,4096]{2,0,1:T(8,128)S(1)} %get-tuple-element.376, f32[256,4]{0,1:T(4,128)S(1)} %get-tuple-element.377, pred[256,4096]{1,0:T(8,128)(4,1)S(1)} %compare_and_fusion.2, f32[256,4,128]{2,0,1:T(8,128)S(1)} %get-tuple-element.401, ...), kind=kOutput, calls=%fused_computation.14.clone.1 | convolution fusion | flops 1095368704 | bytes 19943424 | tf_op jit(solution)/shard_map/while/body/eval_jaxpr/nhk,kd->nhd/dot_general | solution.py:34
  288.7 15.8 %collective-permute-done.2 = f32[256,4]{0,1:T(4,128)S(1)} collective-permute-done((f32[256,4]{0,1:T(4,128)S(1)}, f32[256,4]{0,1:T(4,128)S(1)}, u32[]{:S(2)}, u32[]{:S(2)}) %collective-permute-start.2) | collective-permute-done | bytes 4128 | tf_op jit(solution)/shard_map/while/body/eval_jaxpr/ppermute | solution.py:12
  305.4 12.8 %all-gather.2.cloned.1.call-done = bf16[256,2048]{0,1:T(8,128)(2,1)} async-done(((bf16[256,512]{0,1:T(8,128)(2,1)}), bf16[256,2048]{0,1:T(8,128)(2,1)}) %all-gather.2.cloned.1.call-update) | async-done | bytes 1048592 | tf_op jit(solution)/shard_map/all_gather | solution.py:85
  318.2 12.0 %convolution_convert_fusion = bf16[256,4096]{1,0:T(8,128)(2,1)} fusion(bf16[256,2048]{0,1:T(8,128)(2,1)} %all-gather.2.cloned.1.call-done, bf16[2048,4096]{1,0:T(8,128)(2,1)} %param.11), kind=kOutput, calls=%fused_computation.31 | convolution fusion | flops 4296015872 | bytes 19922944 | tf_op jit(solution)/shard_map/dot_general | solution.py:84
  (113 shorter events, 6.4 us)
Async XLA Ops:
  6.5 311.6 %all-gather.2.cloned.1.call-start = ((), (), s32[]{:S(2)}) async-start(), calls=%async_computation | async-start | bytes 1310720 | tf_op jit(solution)/shard_map/all_gather | solution.py:85
  10.7 9.9 %copy-start = (bf16[4096,128]{1,0:T(8,128)(2,1)S(1)}, bf16[4096,128]{1,0:T(8,128)(2,1)}, u32[]{:S(2)}) copy-start(bf16[4096,128]{1,0:T(8,128)(2,1)} %get-tuple-element.425) | copy-start | bytes 3145732 | tf_op jit(solution)/shard_map/while
  27.0 23.7 %collective-permute-start.1 = (f32[256,4,128]{2,0,1:T(8,128)S(1)}, f32[256,4,128]{2,0,1:T(8,128)S(1)}, u32[]{:S(2)}, u32[]{:S(2)}) collective-permute-start(f32[256,4,128]{2,0,1:T(8,128)S(1)} %fusion.53), channel_id=1, source_target_pairs={{0,4},{4,8},{8,12},{12,16},{16,20},{20,24},{24,28},{28,0},{1,5},{5... | collective-permute-start | bytes 1572872 | tf_op jit(solution)/shard_map/while/body/eval_jaxpr/ppermute | solution.py:12
  30.0 20.7 %collective-permute-start = (bf16[256,512]{1,0:T(8,128)(2,1)S(1)}, bf16[256,512]{1,0:T(8,128)(2,1)S(1)}, u32[]{:S(2)}, u32[]{:S(2)}) collective-permute-start(bf16[256,512]{1,0:T(8,128)(2,1)S(1)} %copy.26), channel_id=1, source_target_pairs={{0,4},{4,8},{8,12},{12,16},{16,20},{20,24},{24,28},{28,0},{1,5},{5... | collective-permute-start | bytes 786440 | tf_op jit(solution)/shard_map/while/body/eval_jaxpr/ppermute | solution.py:12
  31.5 19.1 %collective-permute-start.2 = (f32[256,4]{0,1:T(4,128)S(1)}, f32[256,4]{0,1:T(4,128)S(1)}, u32[]{:S(2)}, u32[]{:S(2)}) collective-permute-start(f32[256,4]{0,1:T(4,128)S(1)} %get-tuple-element.382), channel_id=1, source_target_pairs={{0,4},{4,8},{8,12},{12,16},{16,20},{20,24},{24,28},{28,0},{1,5},{5... | collective-permute-start | bytes 12296 | tf_op jit(solution)/shard_map/while/body/eval_jaxpr/ppermute | solution.py:12
  51.8 9.9 %copy-start = (bf16[4096,128]{1,0:T(8,128)(2,1)S(1)}, bf16[4096,128]{1,0:T(8,128)(2,1)}, u32[]{:S(2)}) copy-start(bf16[4096,128]{1,0:T(8,128)(2,1)} %get-tuple-element.425) | copy-start | bytes 3145732 | tf_op jit(solution)/shard_map/while
  68.1 21.6 %collective-permute-start.1 = (f32[256,4,128]{2,0,1:T(8,128)S(1)}, f32[256,4,128]{2,0,1:T(8,128)S(1)}, u32[]{:S(2)}, u32[]{:S(2)}) collective-permute-start(f32[256,4,128]{2,0,1:T(8,128)S(1)} %fusion.53), channel_id=1, source_target_pairs={{0,4},{4,8},{8,12},{12,16},{16,20},{20,24},{24,28},{28,0},{1,5},{5... | collective-permute-start | bytes 1572872 | tf_op jit(solution)/shard_map/while/body/eval_jaxpr/ppermute | solution.py:12
  68.2 21.5 %collective-permute-start = (bf16[256,512]{1,0:T(8,128)(2,1)S(1)}, bf16[256,512]{1,0:T(8,128)(2,1)S(1)}, u32[]{:S(2)}, u32[]{:S(2)}) collective-permute-start(bf16[256,512]{1,0:T(8,128)(2,1)S(1)} %copy.26), channel_id=1, source_target_pairs={{0,4},{4,8},{8,12},{12,16},{16,20},{20,24},{24,28},{28,0},{1,5},{5... | collective-permute-start | bytes 786440 | tf_op jit(solution)/shard_map/while/body/eval_jaxpr/ppermute | solution.py:12
  69.3 20.4 %collective-permute-start.2 = (f32[256,4]{0,1:T(4,128)S(1)}, f32[256,4]{0,1:T(4,128)S(1)}, u32[]{:S(2)}, u32[]{:S(2)}) collective-permute-start(f32[256,4]{0,1:T(4,128)S(1)} %get-tuple-element.382), channel_id=1, source_target_pairs={{0,4},{4,8},{8,12},{12,16},{16,20},{20,24},{24,28},{28,0},{1,5},{5... | collective-permute-start | bytes 12296 | tf_op jit(solution)/shard_map/while/body/eval_jaxpr/ppermute | solution.py:12
  90.8 9.9 %copy-start = (bf16[4096,128]{1,0:T(8,128)(2,1)S(1)}, bf16[4096,128]{1,0:T(8,128)(2,1)}, u32[]{:S(2)}) copy-start(bf16[4096,128]{1,0:T(8,128)(2,1)} %get-tuple-element.425) | copy-start | bytes 3145732 | tf_op jit(solution)/shard_map/while
  107.2 20.7 %collective-permute-start.1 = (f32[256,4,128]{2,0,1:T(8,128)S(1)}, f32[256,4,128]{2,0,1:T(8,128)S(1)}, u32[]{:S(2)}, u32[]{:S(2)}) collective-permute-start(f32[256,4,128]{2,0,1:T(8,128)S(1)} %fusion.53), channel_id=1, source_target_pairs={{0,4},{4,8},{8,12},{12,16},{16,20},{20,24},{24,28},{28,0},{1,5},{5... | collective-permute-start | bytes 1572872 | tf_op jit(solution)/shard_map/while/body/eval_jaxpr/ppermute | solution.py:12
  107.2 20.6 %collective-permute-start = (bf16[256,512]{1,0:T(8,128)(2,1)S(1)}, bf16[256,512]{1,0:T(8,128)(2,1)S(1)}, u32[]{:S(2)}, u32[]{:S(2)}) collective-permute-start(bf16[256,512]{1,0:T(8,128)(2,1)S(1)} %copy.26), channel_id=1, source_target_pairs={{0,4},{4,8},{8,12},{12,16},{16,20},{20,24},{24,28},{28,0},{1,5},{5... | collective-permute-start | bytes 786440 | tf_op jit(solution)/shard_map/while/body/eval_jaxpr/ppermute | solution.py:12
  107.3 20.5 %collective-permute-start.2 = (f32[256,4]{0,1:T(4,128)S(1)}, f32[256,4]{0,1:T(4,128)S(1)}, u32[]{:S(2)}, u32[]{:S(2)}) collective-permute-start(f32[256,4]{0,1:T(4,128)S(1)} %get-tuple-element.382), channel_id=1, source_target_pairs={{0,4},{4,8},{8,12},{12,16},{16,20},{20,24},{24,28},{28,0},{1,5},{5... | collective-permute-start | bytes 12296 | tf_op jit(solution)/shard_map/while/body/eval_jaxpr/ppermute | solution.py:12
  128.9 9.9 %copy-start = (bf16[4096,128]{1,0:T(8,128)(2,1)S(1)}, bf16[4096,128]{1,0:T(8,128)(2,1)}, u32[]{:S(2)}) copy-start(bf16[4096,128]{1,0:T(8,128)(2,1)} %get-tuple-element.425) | copy-start | bytes 3145732 | tf_op jit(solution)/shard_map/while
  145.3 19.7 %collective-permute-start.1 = (f32[256,4,128]{2,0,1:T(8,128)S(1)}, f32[256,4,128]{2,0,1:T(8,128)S(1)}, u32[]{:S(2)}, u32[]{:S(2)}) collective-permute-start(f32[256,4,128]{2,0,1:T(8,128)S(1)} %fusion.53), channel_id=1, source_target_pairs={{0,4},{4,8},{8,12},{12,16},{16,20},{20,24},{24,28},{28,0},{1,5},{5... | collective-permute-start | bytes 1572872 | tf_op jit(solution)/shard_map/while/body/eval_jaxpr/ppermute | solution.py:12
  145.3 19.7 %collective-permute-start = (bf16[256,512]{1,0:T(8,128)(2,1)S(1)}, bf16[256,512]{1,0:T(8,128)(2,1)S(1)}, u32[]{:S(2)}, u32[]{:S(2)}) collective-permute-start(bf16[256,512]{1,0:T(8,128)(2,1)S(1)} %copy.26), channel_id=1, source_target_pairs={{0,4},{4,8},{8,12},{12,16},{16,20},{20,24},{24,28},{28,0},{1,5},{5... | collective-permute-start | bytes 786440 | tf_op jit(solution)/shard_map/while/body/eval_jaxpr/ppermute | solution.py:12
  145.4 19.6 %collective-permute-start.2 = (f32[256,4]{0,1:T(4,128)S(1)}, f32[256,4]{0,1:T(4,128)S(1)}, u32[]{:S(2)}, u32[]{:S(2)}) collective-permute-start(f32[256,4]{0,1:T(4,128)S(1)} %get-tuple-element.382), channel_id=1, source_target_pairs={{0,4},{4,8},{8,12},{12,16},{16,20},{20,24},{24,28},{28,0},{1,5},{5... | collective-permute-start | bytes 12296 | tf_op jit(solution)/shard_map/while/body/eval_jaxpr/ppermute | solution.py:12
  166.1 9.9 %copy-start = (bf16[4096,128]{1,0:T(8,128)(2,1)S(1)}, bf16[4096,128]{1,0:T(8,128)(2,1)}, u32[]{:S(2)}) copy-start(bf16[4096,128]{1,0:T(8,128)(2,1)} %get-tuple-element.425) | copy-start | bytes 3145732 | tf_op jit(solution)/shard_map/while
  182.5 18.8 %collective-permute-start.1 = (f32[256,4,128]{2,0,1:T(8,128)S(1)}, f32[256,4,128]{2,0,1:T(8,128)S(1)}, u32[]{:S(2)}, u32[]{:S(2)}) collective-permute-start(f32[256,4,128]{2,0,1:T(8,128)S(1)} %fusion.53), channel_id=1, source_target_pairs={{0,4},{4,8},{8,12},{12,16},{16,20},{20,24},{24,28},{28,0},{1,5},{5... | collective-permute-start | bytes 1572872 | tf_op jit(solution)/shard_map/while/body/eval_jaxpr/ppermute | solution.py:12
  182.5 18.7 %collective-permute-start = (bf16[256,512]{1,0:T(8,128)(2,1)S(1)}, bf16[256,512]{1,0:T(8,128)(2,1)S(1)}, u32[]{:S(2)}, u32[]{:S(2)}) collective-permute-start(bf16[256,512]{1,0:T(8,128)(2,1)S(1)} %copy.26), channel_id=1, source_target_pairs={{0,4},{4,8},{8,12},{12,16},{16,20},{20,24},{24,28},{28,0},{1,5},{5... | collective-permute-start | bytes 786440 | tf_op jit(solution)/shard_map/while/body/eval_jaxpr/ppermute | solution.py:12
  182.6 18.7 %collective-permute-start.2 = (f32[256,4]{0,1:T(4,128)S(1)}, f32[256,4]{0,1:T(4,128)S(1)}, u32[]{:S(2)}, u32[]{:S(2)}) collective-permute-start(f32[256,4]{0,1:T(4,128)S(1)} %get-tuple-element.382), channel_id=1, source_target_pairs={{0,4},{4,8},{8,12},{12,16},{16,20},{20,24},{24,28},{28,0},{1,5},{5... | collective-permute-start | bytes 12296 | tf_op jit(solution)/shard_map/while/body/eval_jaxpr/ppermute | solution.py:12
  202.4 9.9 %copy-start = (bf16[4096,128]{1,0:T(8,128)(2,1)S(1)}, bf16[4096,128]{1,0:T(8,128)(2,1)}, u32[]{:S(2)}) copy-start(bf16[4096,128]{1,0:T(8,128)(2,1)} %get-tuple-element.425) | copy-start | bytes 3145732 | tf_op jit(solution)/shard_map/while
  218.7 17.9 %collective-permute-start.1 = (f32[256,4,128]{2,0,1:T(8,128)S(1)}, f32[256,4,128]{2,0,1:T(8,128)S(1)}, u32[]{:S(2)}, u32[]{:S(2)}) collective-permute-start(f32[256,4,128]{2,0,1:T(8,128)S(1)} %fusion.53), channel_id=1, source_target_pairs={{0,4},{4,8},{8,12},{12,16},{16,20},{20,24},{24,28},{28,0},{1,5},{5... | collective-permute-start | bytes 1572872 | tf_op jit(solution)/shard_map/while/body/eval_jaxpr/ppermute | solution.py:12
  218.8 17.8 %collective-permute-start = (bf16[256,512]{1,0:T(8,128)(2,1)S(1)}, bf16[256,512]{1,0:T(8,128)(2,1)S(1)}, u32[]{:S(2)}, u32[]{:S(2)}) collective-permute-start(bf16[256,512]{1,0:T(8,128)(2,1)S(1)} %copy.26), channel_id=1, source_target_pairs={{0,4},{4,8},{8,12},{12,16},{16,20},{20,24},{24,28},{28,0},{1,5},{5... | collective-permute-start | bytes 786440 | tf_op jit(solution)/shard_map/while/body/eval_jaxpr/ppermute | solution.py:12
  218.9 17.7 %collective-permute-start.2 = (f32[256,4]{0,1:T(4,128)S(1)}, f32[256,4]{0,1:T(4,128)S(1)}, u32[]{:S(2)}, u32[]{:S(2)}) collective-permute-start(f32[256,4]{0,1:T(4,128)S(1)} %get-tuple-element.382), channel_id=1, source_target_pairs={{0,4},{4,8},{8,12},{12,16},{16,20},{20,24},{24,28},{28,0},{1,5},{5... | collective-permute-start | bytes 12296 | tf_op jit(solution)/shard_map/while/body/eval_jaxpr/ppermute | solution.py:12
  237.8 9.9 %copy-start = (bf16[4096,128]{1,0:T(8,128)(2,1)S(1)}, bf16[4096,128]{1,0:T(8,128)(2,1)}, u32[]{:S(2)}) copy-start(bf16[4096,128]{1,0:T(8,128)(2,1)} %get-tuple-element.425) | copy-start | bytes 3145732 | tf_op jit(solution)/shard_map/while
  254.1 17.0 %collective-permute-start.1 = (f32[256,4,128]{2,0,1:T(8,128)S(1)}, f32[256,4,128]{2,0,1:T(8,128)S(1)}, u32[]{:S(2)}, u32[]{:S(2)}) collective-permute-start(f32[256,4,128]{2,0,1:T(8,128)S(1)} %fusion.53), channel_id=1, source_target_pairs={{0,4},{4,8},{8,12},{12,16},{16,20},{20,24},{24,28},{28,0},{1,5},{5... | collective-permute-start | bytes 1572872 | tf_op jit(solution)/shard_map/while/body/eval_jaxpr/ppermute | solution.py:12
  254.2 16.9 %collective-permute-start = (bf16[256,512]{1,0:T(8,128)(2,1)S(1)}, bf16[256,512]{1,0:T(8,128)(2,1)S(1)}, u32[]{:S(2)}, u32[]{:S(2)}) collective-permute-start(bf16[256,512]{1,0:T(8,128)(2,1)S(1)} %copy.26), channel_id=1, source_target_pairs={{0,4},{4,8},{8,12},{12,16},{16,20},{20,24},{24,28},{28,0},{1,5},{5... | collective-permute-start | bytes 786440 | tf_op jit(solution)/shard_map/while/body/eval_jaxpr/ppermute | solution.py:12
  254.2 16.8 %collective-permute-start.2 = (f32[256,4]{0,1:T(4,128)S(1)}, f32[256,4]{0,1:T(4,128)S(1)}, u32[]{:S(2)}, u32[]{:S(2)}) collective-permute-start(f32[256,4]{0,1:T(4,128)S(1)} %get-tuple-element.382), channel_id=1, source_target_pairs={{0,4},{4,8},{8,12},{12,16},{16,20},{20,24},{24,28},{28,0},{1,5},{5... | collective-permute-start | bytes 12296 | tf_op jit(solution)/shard_map/while/body/eval_jaxpr/ppermute | solution.py:12
  272.2 9.9 %copy-start = (bf16[4096,128]{1,0:T(8,128)(2,1)S(1)}, bf16[4096,128]{1,0:T(8,128)(2,1)}, u32[]{:S(2)}) copy-start(bf16[4096,128]{1,0:T(8,128)(2,1)} %get-tuple-element.425) | copy-start | bytes 3145732 | tf_op jit(solution)/shard_map/while
  288.5 16.0 %collective-permute-start.1 = (f32[256,4,128]{2,0,1:T(8,128)S(1)}, f32[256,4,128]{2,0,1:T(8,128)S(1)}, u32[]{:S(2)}, u32[]{:S(2)}) collective-permute-start(f32[256,4,128]{2,0,1:T(8,128)S(1)} %fusion.53), channel_id=1, source_target_pairs={{0,4},{4,8},{8,12},{12,16},{16,20},{20,24},{24,28},{28,0},{1,5},{5... | collective-permute-start | bytes 1572872 | tf_op jit(solution)/shard_map/while/body/eval_jaxpr/ppermute | solution.py:12
  288.6 16.0 %collective-permute-start = (bf16[256,512]{1,0:T(8,128)(2,1)S(1)}, bf16[256,512]{1,0:T(8,128)(2,1)S(1)}, u32[]{:S(2)}, u32[]{:S(2)}) collective-permute-start(bf16[256,512]{1,0:T(8,128)(2,1)S(1)} %copy.26), channel_id=1, source_target_pairs={{0,4},{4,8},{8,12},{12,16},{16,20},{20,24},{24,28},{28,0},{1,5},{5... | collective-permute-start | bytes 786440 | tf_op jit(solution)/shard_map/while/body/eval_jaxpr/ppermute | solution.py:12
  288.7 15.9 %collective-permute-start.2 = (f32[256,4]{0,1:T(4,128)S(1)}, f32[256,4]{0,1:T(4,128)S(1)}, u32[]{:S(2)}, u32[]{:S(2)}) collective-permute-start(f32[256,4]{0,1:T(4,128)S(1)} %get-tuple-element.382), channel_id=1, source_target_pairs={{0,4},{4,8},{8,12},{12,16},{16,20},{20,24},{24,28},{28,0},{1,5},{5... | collective-permute-start | bytes 12296 | tf_op jit(solution)/shard_map/while/body/eval_jaxpr/ppermute | solution.py:12
Sparse Core Ops, SparseCore 0:
  305.5 12.5 all-gather.1
where the time goes:
time: 337 us
  waiting for transfers between devices  159 us (47%)
  matrix products  102 us (30%)
  other arithmetic  51.3 us (15%)
  between operations  13.4 us (4%)
  starting transfers between devices  8.86 us (3%)
    ppermute x24, waiting for transfers between devices, from_behind(): return lax.ppermute(value, axis, pairs)  146 us
    dot_general x8, matrix products, partial_block(): jnp.einsum('nhk,kd->nhd', weights.astype(jnp.bfloat16), value_rows, prefe...  51.5 us
    reduce_sum x8, other arithmetic, partial_block(): total = jnp.sum(weights, axis=2)  40.3 us
    dot_general x8, matrix products, partial_block(): jnp.einsum('nhd,kd->nhk', q_three, key_rows, preferred_element_type=jnp.f...  38.3 us
    all_gather x1, waiting for transfers between devices, body(): lax.all_gather(attended, 'head', axis=1, tiled=True)  12.8 us
    dot_general x1, matrix products, body(): jnp.dot(lax.all_gather(attended, 'head', axis=1, tiled=True), w_out, pref...  12 us
    ppermute x24, starting transfers between devices, from_behind(): return lax.ppermute(value, axis, pairs)  8.86 us
    and x8, other arithmetic, partial_block(): (q_req[:, None] == k_req[None, :]) & (k_pos[None, :] <= q_pos[:, None])  7.35 us
  transfers between devices with their start and end apart: 25, of which 9 were waited for; matrix products, arithmetic and copies ran while one was open for 0% of the time, Pallas kernels for 0%

commit v1 on v0

v1 whole, which is shorter than its diff:
```python
import functools
import math

import jax
import jax.numpy as jnp
from jax import lax
from jax.experimental import pallas as pl
from jax.experimental.pallas import tpu as pltpu
from jax.sharding import PartitionSpec as P

NEG = -1e30
CALM = 60.0
ROW_TILE = 128
KEY_TILE = 512
SIDE = 16
LANES = 128
SMEM = pl.BlockSpec(memory_space=pltpu.SMEM)
VMEM = pl.BlockSpec(memory_space=pltpu.VMEM)


def request_table(new_ref, prior_ref):
    table = []
    row, key = jnp.int32(0), jnp.int32(0)
    for request in range(new_ref.shape[0]):
        new, prior = new_ref[request], prior_ref[request]
        table.append((row, key, key + prior - row))
        row, key = row + new, key + new + prior
    return table


def key_range(table, row):
    first = jnp.broadcast_to(table[0][1], jnp.shape(row))
    shift = jnp.broadcast_to(table[0][2], jnp.shape(row))
    for start, key, ahead in table[1:]:
        own = row >= start
        first = jnp.where(own, key, first)
        shift = jnp.where(own, ahead, shift)
    return first, row + shift


def attend_kernel(slots, chunks, *refs):
    new_ref, prior_ref, row_ref, key_ref = refs[:4]
    q_refs = refs[4:4 + slots]
    kt_refs = refs[4 + slots:4 + slots + chunks]
    v_refs = refs[4 + slots + chunks:4 + slots + 2 * chunks]
    out_refs = refs[4 + slots + 2 * chunks:4 + 2 * slots + 2 * chunks]
    q_all, kt_all, va_all, out_all, logs_all, acc, top, qs = refs[4 + 2 * slots + 2 * chunks:]
    rows = q_refs[0].shape[0]
    width, cache = kt_all.shape
    heads = q_refs[0].shape[1] // width
    tile = min(ROW_TILE, rows)
    step = min(KEY_TILE, min(ref.shape[1] for ref in kt_refs))
    per_slot = rows // tile
    scale = width ** (-0.5)
    factor = scale * math.log2(math.e)
    table = request_table(new_ref, prior_ref)

    for slot in range(slots):
        q_all[slot * rows:(slot + 1) * rows, :] = q_refs[slot][...]
    done = 0
    for kt_ref, v_ref in zip(kt_refs, v_refs):
        count = kt_ref.shape[1]
        kt_all[:, done:done + count] = kt_ref[...]
        va_all[done:done + count, :width] = v_ref[...]
        done += count
    va_all[:, width:] = jnp.ones((cache, width), va_all.dtype)

    def key_norm(at, biggest):
        part = kt_all[:, pl.ds(pl.multiple_of(at * step, step), step)].astype(jnp.float32)
        return jnp.maximum(biggest, jnp.sum(part * part, axis=0, keepdims=True))

    def query_norm(at, biggest):
        for head in range(heads):
            part = q_all[pl.ds(pl.multiple_of(at * tile, tile), tile), head * width:(head + 1) * width].astype(jnp.float32)
            biggest = jnp.maximum(biggest, jnp.sum(part * part, axis=1, keepdims=True))
        return biggest

    key_max = jnp.max(lax.fori_loop(0, cache // step, key_norm, jnp.zeros((1, step), jnp.float32)))
    query_max = jnp.max(lax.fori_loop(0, slots * per_slot, query_norm, jnp.zeros((tile, 1), jnp.float32)))
    calm = query_max * key_max * (scale * scale) <= CALM * CALM

    def one_tile(at, carry):
        local = pl.multiple_of(at * tile, tile)
        row = row_ref[lax.div(at, per_slot)] + lax.rem(at, per_slot) * tile
        first_low, last_low = key_range(table, row)
        first_high, last_high = key_range(table, row + (tile - 1))
        acc[...] = jnp.zeros_like(acc)
        for head in range(heads):
            qs[head * tile:(head + 1) * tile, :] = q_all[pl.ds(local, tile), head * width:(head + 1) * width]
        own_rows = row + lax.broadcasted_iota(jnp.int32, (tile, 1), 0)
        first, last = key_range(table, own_rows)

        def allowed(key):
            index = key + lax.broadcasted_iota(jnp.int32, (tile, step), 1)
            return (index >= first) & (index <= last)

        def scores(part, left):
            return jnp.dot(qs[part, :], kt_all[:, pl.ds(left, step)], preferred_element_type=jnp.float32) * factor

        def add(left, weights):
            return jnp.dot(
                weights.astype(jnp.bfloat16), va_all[pl.ds(left, step), :], preferred_element_type=jnp.float32
            )

        @pl.when(calm)
        def _():
            def turn(at_key, carry):
                left = pl.multiple_of(at_key * step, step)
                key = key_ref[at_key]
                some = (key + step > first_low) & (key <= last_high)
                whole = (key >= first_high) & (key + step - 1 <= last_low)

                @pl.when(whole)
                def _():
                    acc[...] += add(left, jnp.exp2(scores(slice(None), left)))

                @pl.when(some & jnp.logical_not(whole))
                def _():
                    mask = allowed(key)
                    for head in range(heads):
                        part = slice(head * tile, (head + 1) * tile)
                        acc[part, :] += add(left, jnp.where(mask, jnp.exp2(scores(part, left)), 0.0))

                return carry

            lax.fori_loop(0, cache // step, turn, 0)
            top[...] = jnp.zeros_like(top)

        @pl.when(jnp.logical_not(calm))
        def _():
            top[...] = jnp.full_like(top, NEG)

            def turn(at_key, carry):
                left = pl.multiple_of(at_key * step, step)
                key = key_ref[at_key]

                @pl.when((key + step > first_low) & (key <= last_high))
                def _():
                    mask = allowed(key)
                    for head in range(heads):
                        part = slice(head * tile, (head + 1) * tile)
                        score = jnp.where(mask, scores(part, left), NEG)
                        old = top[part, :]
                        new = jnp.maximum(old, jnp.max(score, axis=1, keepdims=True))
                        weights = jnp.where(mask, jnp.exp2(score - new[:, :1]), 0.0)
                        shrink = jnp.exp2(old - new)
                        acc[part, :width] = acc[part, :width] * shrink
                        acc[part, width:] = acc[part, width:] * shrink
                        acc[part, :] += add(left, weights)
                        top[part, :] = new

                return carry

            lax.fori_loop(0, cache // step, turn, 0)

        lane = lax.broadcasted_iota(jnp.int32, (tile, LANES), 1)
        logs = jnp.zeros((tile, LANES), jnp.float32)
        for head in range(heads):
            part = slice(head * tile, (head + 1) * tile)
            total = acc[part, width:]
            live = total > 0.0
            safe = jnp.where(live, total, 1.0)
            out_all[pl.ds(local, tile), head * width:(head + 1) * width] = (acc[part, :width] / safe).astype(jnp.bfloat16)
            logs = jnp.where(lax.rem(lane, heads) == head, jnp.where(live, top[part, :] + jnp.log2(safe), NEG), logs)
        high = logs.astype(jnp.bfloat16).astype(jnp.float32)
        middle = (logs - high).astype(jnp.bfloat16).astype(jnp.float32)
        logs_all[pl.ds(local, tile), :] = jnp.where(
            lane < heads, high, jnp.where(lane < 2 * heads, middle, logs - high - middle)
        )
        return carry

    lax.fori_loop(0, slots * per_slot, one_tile, 0)
    for slot in range(slots):
        out_refs[slot][:rows, :] = out_all[slot * rows:(slot + 1) * rows, :]
        out_refs[slot][rows:, :] = jnp.zeros((SIDE, heads * width), jnp.bfloat16)
        for at in range(0, rows, LANES):
            turned = logs_all[slot * rows + at:slot * rows + at + LANES, :].T
            out_refs[slot][rows:, at:at + LANES] = turned[:SIDE, :].astype(jnp.bfloat16)


def attend(queries, turned_keys, values, new_counts, prior_lengths, row_starts, key_starts):
    slots, chunks = len(queries), len(turned_keys)
    rows = queries[0].shape[0]
    width = values[0].shape[1]
    cache = sum(part.shape[0] for part in values)
    heads = queries[0].shape[1] // width
    tile = min(ROW_TILE, rows)
    return pl.pallas_call(
        functools.partial(attend_kernel, slots, chunks),
        out_shape=tuple(jax.ShapeDtypeStruct((rows + SIDE, heads * width), jnp.bfloat16) for _ in range(slots)),
        in_specs=[SMEM] * 4 + [VMEM] * (slots + 2 * chunks),
        out_specs=(VMEM,) * slots,
        scratch_shapes=[
            pltpu.VMEM((slots * rows, heads * width), jnp.bfloat16),
            pltpu.VMEM((width, cache), jnp.bfloat16),
            pltpu.VMEM((cache, 2 * width), jnp.bfloat16),
            pltpu.VMEM((slots * rows, heads * width), jnp.bfloat16),
            pltpu.VMEM((slots * rows, LANES), jnp.float32),
            pltpu.VMEM((heads * tile, 2 * width), jnp.float32),
            pltpu.VMEM((heads * tile, width), jnp.float32),
            pltpu.VMEM((heads * tile, width), jnp.bfloat16),
        ],
        compiler_params=pltpu.CompilerParams(vmem_limit_bytes=36 * 1024 * 1024),
        cost_estimate=pl.CostEstimate(
            flops=slots * rows * heads * cache * width * 2, bytes_accessed=8 * 1024 * 1024, transcendentals=0
        ),
        name="attend",
    )(new_counts, prior_lengths, row_starts, key_starts, *queries, *turned_keys, *values)


def merge_kernel(heads, *refs):
    parts, out_ref = refs[:-1], refs[-1]
    rows = out_ref.shape[0]
    width = out_ref.shape[1] // heads
    logs = [part[rows:, :rows].astype(jnp.float32) for part in parts]
    spare = LANES - SIDE * len(parts)
    if spare:
        logs.append(jnp.full((spare, rows), NEG, jnp.float32))
    terms = jnp.concatenate(logs, axis=0).T
    total = terms + pltpu.roll(terms, LANES - heads, 1) + pltpu.roll(terms, LANES - 2 * heads, 1)
    lane = lax.broadcasted_iota(jnp.int32, (rows, LANES), 1)
    total = jnp.where((lax.rem(lane, SIDE) < heads) & (lane < SIDE * len(parts)), total, NEG)
    biggest = total
    for shift in (16, 32, 64):
        biggest = jnp.maximum(biggest, pltpu.roll(biggest, shift, 1))
    share = jnp.exp2(total - biggest)
    weight = share
    for shift in (16, 32, 64):
        weight = weight + pltpu.roll(weight, shift, 1)
    share = share / weight
    for head in range(heads):
        own = slice(head * width, (head + 1) * width)
        mixed = jnp.zeros((rows, width), jnp.float32)
        for at, part in enumerate(parts):
            lane_at = at * SIDE + head
            mixed = mixed + part[:rows, own].astype(jnp.float32) * share[:, lane_at:lane_at + 1]
        out_ref[:, own] = mixed.astype(out_ref.dtype)


def merge(parts, heads):
    rows = parts[0].shape[0] - SIDE
    return pl.pallas_call(
        functools.partial(merge_kernel, heads),
        out_shape=jax.ShapeDtypeStruct((rows, parts[0].shape[1]), jnp.bfloat16),
        in_specs=[VMEM] * len(parts),
        out_specs=VMEM,
        compiler_params=pltpu.CompilerParams(vmem_limit_bytes=16 * 1024 * 1024),
        name="merge",
    )(*parts)


def project_kernel(pieces, at_ref, *refs):
    w_ref, out_ref = refs[pieces], refs[pieces + 1]
    deep = refs[0].shape[1]
    total = None
    for at, piece in enumerate(refs[:pieces]):
        start = pl.multiple_of(at_ref[at] * deep, deep)
        term = jnp.dot(piece[...], w_ref[pl.ds(start, deep), :], preferred_element_type=jnp.float32)
        total = term if total is None else total + term
    out_ref[...] = total.astype(out_ref.dtype)


def project(pieces, places, w_out):
    rows, deep = pieces[0].shape
    depth, wide = w_out.shape
    block = min(512, wide)
    return pl.pallas_call(
        functools.partial(project_kernel, len(pieces)),
        out_shape=jax.ShapeDtypeStruct((rows, wide), jnp.bfloat16),
        grid=(wide // block,),
        in_specs=[SMEM]
        + [pl.BlockSpec((rows, deep), lambda at: (0, 0))] * len(pieces)
        + [pl.BlockSpec((depth, block), lambda at: (0, at))],
        out_specs=pl.BlockSpec((rows, block), lambda at: (0, at)),
        compiler_params=pltpu.CompilerParams(vmem_limit_bytes=24 * 1024 * 1024),
        cost_estimate=pl.CostEstimate(
            flops=2 * rows * depth * wide, bytes_accessed=2 * depth * wide, transcendentals=0
        ),
        name="project",
    )(places, *pieces, w_out)


def shift_pairs(count, stride, steps):
    groups = count // stride
    return [
        (group * stride + member, (group + steps) % groups * stride + member)
        for group in range(groups)
        for member in range(stride)
    ]


def swap_pairs(count):
    return [(at, at ^ 1) for at in range(count)]


def body(queries, keys, values, w_out, new_counts, prior_lengths):
    ctx_count, head_count = lax.axis_size("ctx"), lax.axis_size("head")
    device, place = lax.axis_index("ctx"), lax.axis_index("head")
    rows = queries.shape[0]
    cache, width = keys.shape
    heads = queries.shape[1] // width
    groups, half = ctx_count // 2, cache // 2
    group, side, core = device // 2, device % 2, place % 2

    blocks = [queries] + [
        lax.ppermute(queries, "ctx", shift_pairs(ctx_count, 2, steps)) for steps in range(1, groups)
    ]
    row_starts = jnp.stack([(((group - steps) % groups) * 2 + side) * rows for steps in range(groups)]).astype(jnp.int32)

    turned = keys.T
    part_k = lax.dynamic_slice_in_dim(turned, core * half, half, axis=1)
    part_v = lax.dynamic_slice_in_dim(values, core * half, half, axis=0)
    got_k = lax.ppermute(part_k, "ctx", swap_pairs(ctx_count))
    got_v = lax.ppermute(part_v, "ctx", swap_pairs(ctx_count))
    rest_k = lax.ppermute(got_k, "head", swap_pairs(head_count))
    rest_v = lax.ppermute(got_v, "head", swap_pairs(head_count))
    step = min(KEY_TILE, half)
    own_start = device * cache
    other_start = (device ^ 1) * cache
    key_starts = jnp.concatenate([
        own_start + jnp.arange(0, cache, step),
        other_start + core * half + jnp.arange(0, half, step),
        other_start + (1 - core) * half + jnp.arange(0, half, step),
    ]).astype(jnp.int32)

    parts = attend(
        blocks, [turned, got_k, rest_k], [values, got_v, rest_v], new_counts, prior_lengths, row_starts, key_starts
    )
    back = [parts[0]] + [
        lax.ppermute(parts[steps], "ctx", shift_pairs(ctx_count, 2, groups - steps)) for steps in range(1, groups)
    ]
    attended = merge(back, heads)

    chips = head_count // 2
    near = [attended] + [
        lax.ppermute(attended, "head", shift_pairs(head_count, 2, steps)) for steps in range(1, chips)
    ]
    far = [lax.ppermute(piece, "head", swap_pairs(head_count)) for piece in near]
    chip = place // 2
    near_at = [((chip - steps) % chips) * 2 + core for steps in range(chips)]
    far_at = [((chip - steps) % chips) * 2 + (1 - core) for steps in range(chips)]
    return project(near + far, jnp.stack(near_at + far_at).astype(jnp.int32), w_out)


def solution(mesh):
    return jax.shard_map(
        body,
        mesh=mesh,
        in_specs=(P("ctx", "head"), P("ctx", None), P("ctx", None), P(None, "head"), P(), P()),
        out_specs=P("ctx", "head"),
        check_vma=False,
    )
```

time: 337 us -> 211 us (0.63)
  Pallas kernels: 0 us -> 106 us
  matrix products: 102 us -> 0 us
  waiting for transfers between devices: 159 us -> 69.5 us
  other arithmetic: 51.3 us -> 0.24 us
  starting transfers between devices: 8.86 us -> 22.3 us
  between operations: 13.4 us -> 0.06 us
  local copies, waits for them, and re-layouts: 2.02 us -> 11.9 us
    pallas_call x0 -> x3, Pallas kernels: none -> 106 us  [the longest x1 96.9 us: attend(): pl.pallas_call(functools.partial(attend_kernel, slots, chunks), out_shape...]
    dot_general x17 -> x0, matrix products: 102 us -> none  [the longest x8 51.5 us: partial_block(): jnp.einsum('nhk,kd->nhd', weights.astype(jnp.bfloat16), value_rows, prefe...]
    ppermute x24 -> x13, waiting for transfers between devices: 146 us -> 69.5 us  [the longest x3 24.5 us: body(): lax.ppermute(parts[steps], 'ctx', shift_pairs(ctx_count, 2, groups - steps))]
    reduce_sum x26 -> x0, other arithmetic: 41.9 us -> none  [the longest x8 40.3 us: partial_block(): total = jnp.sum(weights, axis=2)]
    ppermute x24 -> x13, starting transfers between devices: 8.86 us -> 22.3 us  [the longest x3 11 us: body(): lax.ppermute(parts[steps], 'ctx', shift_pairs(ctx_count, 2, groups - steps))]
    all_gather x1 -> x0, waiting for transfers between devices: 12.8 us -> none  [body(): lax.all_gather(attended, 'head', axis=1, tiled=True)]
    unnamed x1 -> x11, local copies, waits for them, and re-layouts: 0.95 us -> 10.7 us
    and x8 -> x0, other arithmetic: 7.35 us -> none  [partial_block(): (q_req[:, None] == k_req[None, :]) & (k_pos[None, :] <= q_pos[:, None])]
  transfers between devices with their start and end apart: 25 -> 13, of which waited for: 9 -> 8; matrix products, arithmetic and copies ran while one was open for 0% -> 1% of each run, Pallas kernels for 0% -> 0%
where the time goes in v1:
time: 211 us; the launch traced here: 210 us
  Pallas kernels  106 us (50%)
  waiting for transfers between devices  69.5 us (33%)
  starting transfers between devices  22.3 us (11%)
  local copies, waits for them, and re-layouts  11.9 us (6%)
    pallas_call x1, Pallas kernels, attend(): pl.pallas_call(functools.partial(attend_kernel, slots, chunks), out_shape...  96.9 us
    ppermute x3, waiting for transfers between devices, body(): lax.ppermute(parts[steps], 'ctx', shift_pairs(ctx_count, 2, groups - steps))  24.5 us
    ppermute x3, waiting for transfers between devices, body(): lax.ppermute(queries, 'ctx', shift_pairs(ctx_count, 2, steps))  16.1 us
    ppermute x1, waiting for transfers between devices, body(): got_v = lax.ppermute(part_v, 'ctx', swap_pairs(ctx_count))  11.1 us
    ppermute x3, starting transfers between devices, body(): lax.ppermute(parts[steps], 'ctx', shift_pairs(ctx_count, 2, groups - steps))  11 us
    unnamed x11, local copies, waits for them, and re-layouts  10.7 us
    ppermute x1, waiting for transfers between devices, body(): got_k = lax.ppermute(part_k, 'ctx', swap_pairs(ctx_count))  10.4 us
    pallas_call x1, Pallas kernels, project(): pl.pallas_call(functools.partial(project_kernel, len(pieces)), out_shape=...  8.24 us
  transfers between devices with their start and end apart: 13, of which 8 were waited for; matrix products, arithmetic and copies ran while one was open for 1% of the time, Pallas kernels for 0%

profile of v1, /device:TPU:0, one launch (start us, length us, event | category | flops | bytes accessed | tf_op | source)
XLA Modules:
  0.0 210.5 jit_solution(18236405197194706605)
XLA Ops:
  0.0 1.1 constant_dynamic-slice_fusion
  1.1 3.0 %collective-permute-start.5 = (bf16[2048,128]{1,0:T(8,128)(2,1)S(1)}, bf16[2048,128]{1,0:T(8,128)(2,1)S(1)}, u32[]{:S(2)}, u32[]{:S(2)}) collective-permute-start(bf16[2048,128]{1,0:T(8,128)(2,1)S(1)} %constant_dynamic-slice_fusion), channel_id=1, source_target_pairs={{0,4},{4,0},{8,12},{12,8},{16,20},{20,16},{24,28},{28,24},{1,5},{5... | collective-permute-start | bytes 1572872 | tf_op jit(solution)/shard_map/ppermute | solution.py:314
  4.1 1.5 copy.7
  5.6 0.1 collective-permute-start.3
  5.7 11.1 %collective-permute-done.5.refs_12_ = bf16[2048,128]{1,0:T(8,128)(2,1)S(1)} collective-permute-done((bf16[2048,128]{1,0:T(8,128)(2,1)S(1)}, bf16[2048,128]{1,0:T(8,128)(2,1)S(1)}, u32[]{:S(2)}, u32[]{:S(2)}) %collective-permute-start.5) | collective-permute-done | bytes 524320 | tf_op jit(solution)/shard_map/ppermute | solution.py:314
  16.8 0.0 collective-permute-start.6
  16.8 10.4 %collective-permute-done.3.refs_9_ = bf16[128,2048]{1,0:T(8,128)(2,1)S(1)} collective-permute-done((bf16[128,2048]{1,0:T(8,128)(2,1)S(1)}, bf16[128,2048]{1,0:T(8,128)(2,1)S(1)}, u32[]{:S(2)}, u32[]{:S(2)}) %collective-permute-start.3) | collective-permute-done | bytes 524320 | tf_op jit(solution)/shard_map/ppermute | solution.py:313
  27.2 0.0 collective-permute-start.4
  27.2 2.8 %collective-permute-start.1 = (bf16[256,512]{1,0:T(8,128)(2,1)}, bf16[256,512]{1,0:T(8,128)(2,1)S(1)}, u32[]{:S(2)}, u32[]{:S(2)}) collective-permute-start(bf16[256,512]{1,0:T(8,128)(2,1)} %refs_4_.2), channel_id=1, source_target_pairs={{0,16},{4,20},{8,24},{12,28},{16,0},{20,4},{24,8},{28,12},{1,17},{... | collective-permute-start | bytes 786440 | tf_op jit(solution)/shard_map/ppermute | solution.py:306
  30.1 1.6 collective-permute-start
  31.7 2.2 %collective-permute-start.2 = (bf16[256,512]{1,0:T(8,128)(2,1)}, bf16[256,512]{1,0:T(8,128)(2,1)}, u32[]{:S(2)}, u32[]{:S(2)}) collective-permute-start(bf16[256,512]{1,0:T(8,128)(2,1)} %refs_4_.2), channel_id=1, source_target_pairs={{0,24},{4,28},{8,0},{12,4},{16,8},{20,12},{24,16},{28,20},{1,25},{... | collective-permute-start | bytes 786440 | tf_op jit(solution)/shard_map/ppermute | solution.py:306
  33.9 0.1 pad_add_fusion.2.refs_3_
  34.0 0.1 pad_add_fusion.1.refs_2_
  34.1 14.7 %collective-permute-done.1.refs_6_ = bf16[256,512]{1,0:T(8,128)(2,1)S(1)} collective-permute-done((bf16[256,512]{1,0:T(8,128)(2,1)}, bf16[256,512]{1,0:T(8,128)(2,1)S(1)}, u32[]{:S(2)}, u32[]{:S(2)}) %collective-permute-start.1) | collective-permute-done | bytes 262176 | tf_op jit(solution)/shard_map/ppermute | solution.py:306
  48.8 0.0 collective-permute-done.refs_5_
  48.8 1.4 collective-permute-done.2.refs_7_
  50.2 0.0 collective-permute-done.6.refs_13_
  50.2 0.0 collective-permute-done.4.refs_10_
  50.2 0.0 copy-start.1
  50.2 1.2 copy-done.1
  51.4 0.0 copy-start.2
  51.4 0.9 copy-done.2
  52.4 0.0 copy-start.3
  52.4 0.7 copy-done.3
  53.0 0.0 copy-start.4
  53.0 0.7 copy-done.4
  53.7 96.9 %attend.1 = (bf16[272,512]{1,0:T(8,128)(2,1)S(1)}, bf16[272,512]{1,0:T(8,128)(2,1)S(1)}, bf16[272,512]{1,0:T(8,128)(2,1)S(1)}, bf16[272,512]{1,0:T(8,128)(2,1)S(1)}) custom-call(s32[8]{0:T(128)S(1)} %copy-done.3, s32[8]{0:T(128)S(1)} %copy-done.4, s32[4]{0:T(128)S(1)} %pad_add_fusion.1.refs_2_, s32[16]{0:T(128)S(1)} %pad_add_fusion.2.refs_3_, ...), custom_call_target="tpu_custom_call" | custom-call | flops 8589934592 | bytes 8388608 | tf_op jit(solution)/shard_map/attend/pallas_call | solution.py:188
  150.6 0.1 collective-permute-start.7
  150.7 10.9 %collective-permute-start.8 = (bf16[272,512]{1,0:T(8,128)(2,1)S(1)}, bf16[272,512]{1,0:T(8,128)(2,1)S(1)}, u32[]{:S(2)}, u32[]{:S(2)}) collective-permute-start(bf16[272,512]{1,0:T(8,128)(2,1)S(1)} %get-tuple-element.11), channel_id=1, source_target_pairs={{0,16},{4,20},{8,24},{12,28},{16,0},{20,4},{24,8},{28,12},{1,17},{... | collective-permute-start | bytes 835592 | tf_op jit(solution)/shard_map/ppermute | solution.py:330
  161.6 0.0 collective-permute-start.9
  161.6 5.4 %collective-permute-done.7.refs_1_ = bf16[272,512]{1,0:T(8,128)(2,1)S(1)} collective-permute-done((bf16[272,512]{1,0:T(8,128)(2,1)S(1)}, bf16[272,512]{1,0:T(8,128)(2,1)S(1)}, u32[]{:S(2)}, u32[]{:S(2)}) %collective-permute-start.7) | collective-permute-done | bytes 278560 | tf_op jit(solution)/shard_map/ppermute | solution.py:330
  167.0 19.1 %collective-permute-done.8.refs_2_ = bf16[272,512]{1,0:T(8,128)(2,1)S(1)} collective-permute-done((bf16[272,512]{1,0:T(8,128)(2,1)S(1)}, bf16[272,512]{1,0:T(8,128)(2,1)S(1)}, u32[]{:S(2)}, u32[]{:S(2)}) %collective-permute-start.8) | collective-permute-done | bytes 278560 | tf_op jit(solution)/shard_map/ppermute | solution.py:330
  186.1 0.0 collective-permute-done.9.refs_3_
  186.1 1.3 merge.1.refs_0_
  187.4 1.6 collective-permute-start.10
  189.0 0.0 collective-permute-start.11
  189.0 5.9 %collective-permute-done.10.refs_1_ = bf16[256,512]{1,0:T(8,128)(2,1)S(1)} collective-permute-done((bf16[256,512]{1,0:T(8,128)(2,1)S(1)}, bf16[256,512]{1,0:T(8,128)(2,1)S(1)}, u32[]{:S(2)}, u32[]{:S(2)}) %collective-permute-start.10) | collective-permute-done | bytes 262176 | tf_op jit(solution)/shard_map/ppermute | solution.py:336
  194.9 0.0 collective-permute-start.12
  194.9 0.1 pad_add_fusion.at_ref
  195.0 0.0 collective-permute-done.11.refs_2_
  195.0 1.5 collective-permute-done.12.refs_3_
  196.5 0.0 copy-start
  196.5 5.8 %copy-done = bf16[2048,4096]{1,0:T(8,128)(2,1)S(1)} copy-done((bf16[2048,4096]{1,0:T(8,128)(2,1)S(1)}, bf16[2048,4096]{1,0:T(8,128)(2,1)}, u32[]{:S(2)}) %copy-start) | copy-done | bytes 16777240
  202.2 8.2 %project.1 = bf16[256,4096]{1,0:T(8,128)(2,1)} custom-call(s32[4]{0:T(128)S(1)} %pad_add_fusion.at_ref, bf16[256,512]{1,0:T(8,128)(2,1)S(1)} %merge.1.refs_0_, bf16[256,512]{1,0:T(8,128)(2,1)S(1)} %collective-permute-done.10.refs_1_, bf16[256,512]{1,0:T(8,128)(2,1)S(1)} %collective-permute-done.11.refs_2_, ...), custom_call_target="tpu_custom_call" | custom-call | flops 4294967296 | bytes 16777216 | tf_op jit(solution)/shard_map/project/pallas_call | solution.py:267
  (3 shorter events, 0.1 us)
Async XLA Ops:
  1.1 15.8 %collective-permute-start.5 = (bf16[2048,128]{1,0:T(8,128)(2,1)S(1)}, bf16[2048,128]{1,0:T(8,128)(2,1)S(1)}, u32[]{:S(2)}, u32[]{:S(2)}) collective-permute-start(bf16[2048,128]{1,0:T(8,128)(2,1)S(1)} %constant_dynamic-slice_fusion), channel_id=1, source_target_pairs={{0,4},{4,0},{8,12},{12,8},{16,20},{20,16},{24,28},{28,24},{1,5},{5... | collective-permute-start | bytes 1572872 | tf_op jit(solution)/shard_map/ppermute | solution.py:314
  5.6 21.6 %collective-permute-start.3 = (bf16[128,2048]{1,0:T(8,128)(2,1)S(1)}, bf16[128,2048]{1,0:T(8,128)(2,1)S(1)}, u32[]{:S(2)}, u32[]{:S(2)}) collective-permute-start(bf16[128,2048]{1,0:T(8,128)(2,1)S(1)} %dynamic-slice_bitcast_fusion), channel_id=1, source_target_pairs={{0,4},{4,0},{8,12},{12,8},{16,20},{20,16},{24,28},{28,24},{1,5},{5... | collective-permute-start | bytes 1572872 | tf_op jit(solution)/shard_map/ppermute | solution.py:313
  16.8 33.4 %collective-permute-start.6 = (bf16[2048,128]{1,0:T(8,128)(2,1)S(1)}, bf16[2048,128]{1,0:T(8,128)(2,1)S(1)}, u32[]{:S(2)}, u32[]{:S(2)}) collective-permute-start(bf16[2048,128]{1,0:T(8,128)(2,1)S(1)} %collective-permute-done.5.refs_12_), channel_id=1, source_target_pairs={{0,1},{1,0},{2,3},{3,2},{4,5},{5,4},{6,7},{7,6},{8,9},{9,8},{10,11... | collective-permute-start | bytes 1572872 | tf_op jit(solution)/shard_map/ppermute | solution.py:316
  27.2 23.0 %collective-permute-start.4 = (bf16[128,2048]{1,0:T(8,128)(2,1)S(1)}, bf16[128,2048]{1,0:T(8,128)(2,1)S(1)}, u32[]{:S(2)}, u32[]{:S(2)}) collective-permute-start(bf16[128,2048]{1,0:T(8,128)(2,1)S(1)} %collective-permute-done.3.refs_9_), channel_id=1, source_target_pairs={{0,1},{1,0},{2,3},{3,2},{4,5},{5,4},{6,7},{7,6},{8,9},{9,8},{10,11... | collective-permute-start | bytes 1572872 | tf_op jit(solution)/shard_map/ppermute | solution.py:315
  27.2 21.6 %collective-permute-start.1 = (bf16[256,512]{1,0:T(8,128)(2,1)}, bf16[256,512]{1,0:T(8,128)(2,1)S(1)}, u32[]{:S(2)}, u32[]{:S(2)}) collective-permute-start(bf16[256,512]{1,0:T(8,128)(2,1)} %refs_4_.2), channel_id=1, source_target_pairs={{0,16},{4,20},{8,24},{12,28},{16,0},{20,4},{24,8},{28,12},{1,17},{... | collective-permute-start | bytes 786440 | tf_op jit(solution)/shard_map/ppermute | solution.py:306
  30.1 18.7 %collective-permute-start = (bf16[256,512]{1,0:T(8,128)(2,1)}, bf16[256,512]{1,0:T(8,128)(2,1)}, u32[]{:S(2)}, u32[]{:S(2)}) collective-permute-start(bf16[256,512]{1,0:T(8,128)(2,1)} %refs_4_.2), channel_id=1, source_target_pairs={{0,8},{4,12},{8,16},{12,20},{16,24},{20,28},{24,0},{28,4},{1,9},{5... | collective-permute-start | bytes 786440 | tf_op jit(solution)/shard_map/ppermute | solution.py:306
  31.7 18.5 %collective-permute-start.2 = (bf16[256,512]{1,0:T(8,128)(2,1)}, bf16[256,512]{1,0:T(8,128)(2,1)}, u32[]{:S(2)}, u32[]{:S(2)}) collective-permute-start(bf16[256,512]{1,0:T(8,128)(2,1)} %refs_4_.2), channel_id=1, source_target_pairs={{0,24},{4,28},{8,0},{12,4},{16,8},{20,12},{24,16},{28,20},{1,25},{... | collective-permute-start | bytes 786440 | tf_op jit(solution)/shard_map/ppermute | solution.py:306
  50.2 1.2 copy-start.1
  51.4 0.9 copy-start.2
  52.4 0.7 copy-start.3
  53.0 0.7 copy-start.4
  150.6 16.4 %collective-permute-start.7 = (bf16[272,512]{1,0:T(8,128)(2,1)S(1)}, bf16[272,512]{1,0:T(8,128)(2,1)S(1)}, u32[]{:S(2)}, u32[]{:S(2)}) collective-permute-start(bf16[272,512]{1,0:T(8,128)(2,1)S(1)} %get-tuple-element.10), channel_id=1, source_target_pairs={{0,24},{4,28},{8,0},{12,4},{16,8},{20,12},{24,16},{28,20},{1,25},{... | collective-permute-start | bytes 835592 | tf_op jit(solution)/shard_map/ppermute | solution.py:330
  150.7 35.4 %collective-permute-start.8 = (bf16[272,512]{1,0:T(8,128)(2,1)S(1)}, bf16[272,512]{1,0:T(8,128)(2,1)S(1)}, u32[]{:S(2)}, u32[]{:S(2)}) collective-permute-start(bf16[272,512]{1,0:T(8,128)(2,1)S(1)} %get-tuple-element.11), channel_id=1, source_target_pairs={{0,16},{4,20},{8,24},{12,28},{16,0},{20,4},{24,8},{28,12},{1,17},{... | collective-permute-start | bytes 835592 | tf_op jit(solution)/shard_map/ppermute | solution.py:330
  161.6 24.5 %collective-permute-start.9 = (bf16[272,512]{1,0:T(8,128)(2,1)S(1)}, bf16[272,512]{1,0:T(8,128)(2,1)S(1)}, u32[]{:S(2)}, u32[]{:S(2)}) collective-permute-start(bf16[272,512]{1,0:T(8,128)(2,1)S(1)} %get-tuple-element.12), channel_id=1, source_target_pairs={{0,8},{4,12},{8,16},{12,20},{16,24},{20,28},{24,0},{28,4},{1,9},{5... | collective-permute-start | bytes 835592 | tf_op jit(solution)/shard_map/ppermute | solution.py:330
  187.4 7.5 %collective-permute-start.10 = (bf16[256,512]{1,0:T(8,128)(2,1)S(1)}, bf16[256,512]{1,0:T(8,128)(2,1)S(1)}, u32[]{:S(2)}, u32[]{:S(2)}) collective-permute-start(bf16[256,512]{1,0:T(8,128)(2,1)S(1)} %merge.1.refs_0_), channel_id=1, source_target_pairs={{0,2},{1,3},{2,0},{3,1},{4,6},{5,7},{6,4},{7,5},{8,10},{9,11},{10,... | collective-permute-start | bytes 786440 | tf_op jit(solution)/shard_map/ppermute | solution.py:336
  189.0 6.0 %collective-permute-start.11 = (bf16[256,512]{1,0:T(8,128)(2,1)S(1)}, bf16[256,512]{1,0:T(8,128)(2,1)S(1)}, u32[]{:S(2)}, u32[]{:S(2)}) collective-permute-start(bf16[256,512]{1,0:T(8,128)(2,1)S(1)} %merge.1.refs_0_), channel_id=1, source_target_pairs={{0,1},{1,0},{2,3},{3,2},{4,5},{5,4},{6,7},{7,6},{8,9},{9,8},{10,11... | collective-permute-start | bytes 786440 | tf_op jit(solution)/shard_map/ppermute | solution.py:338
  194.9 1.5 collective-permute-start.12
  196.5 5.8 %copy-start = (bf16[2048,4096]{1,0:T(8,128)(2,1)S(1)}, bf16[2048,4096]{1,0:T(8,128)(2,1)}, u32[]{:S(2)}) copy-start(bf16[2048,4096]{1,0:T(8,128)(2,1)} %refs_4_.3) | copy-start | bytes 50331652
